TPU v7x, 32 devices: a whole 2x2x4 slice. The times are simulated.
32 devices in a mesh: parts: 2 (over y), space: 4 (over z), dp: 2 (over x), chan: 2 (over core).
Axes of the slice: x: 2, y: 2, z: 4, core: 2. Of those that a mesh axis runs over, the one named last changes fastest.
Arguments:
- features: bfloat16 [4, 16, 64, 512], P(('parts', 'dp'), 'space'), parts along dimension 0, may hold values from -17 to 17
- cotangent: bfloat16 [4, 16, 64, 512], P(('parts', 'dp'), 'space', None, 'chan'), parts along dimension 0, may hold values from -6 to 6
- valid: int32 [4, 16, 64], P(('parts', 'dp'), 'space'), parts along dimension 0, may hold values from 0 to 1, as said below
- coefficients: bfloat16 [64, 8192], P(None, ('dp', 'chan')), may hold values from -0.046875 to 0.046875
Outputs:
- conv_out: bfloat16 [4, 16, 64, 512], P(('parts', 'dp'), 'space', None, 'chan'), parts along dimension 0
- input_grad: bfloat16 [4, 16, 64, 512], P(('parts', 'dp'), 'space', None, 'chan'), parts along dimension 0
- coef_grad: float32 [128, 8192], P(('parts', 'chan'), ('space', 'dp')), parts along dimension 0
There are 2 independent parts, one for each index of `parts`. A program takes and returns all parts, laid end to end along the dimension named above; an argument that names none is the same for every part. Nothing has to cross between parts.
Inputs may be any that keep to these rules, and one draw needn't show every extreme that they name: `valid`: 1 marks a pixel whose loss counts.
All inputs are finite; a program needn't handle non-finite values.
Results may differ from a plain program's by a relative error of at most 0.009.
Values may be sent and summed in bfloat16 or wider, within the bound.
A program may use at most 128 MiB of HBM per device.

v0:
```python
import functools
import math

import jax
import jax.numpy as jnp
import numpy as np
from jax import lax
from jax.experimental import pallas as pl
from jax.experimental.pallas import tpu as pltpu
from jax.sharding import PartitionSpec as P

FIELDS = 64
NB = 16


def padded_2(array, sides, width):
    for axis, dim in sides:
        size, length = (lax.axis_size(axis), array.shape[dim])
        up = [(i, (i + 1) % size) for i in range(size - 1)]
        down = [(j, i) for i, j in up]
        last = lax.slice_in_dim(array, length - width, length, axis=dim)
        first = lax.slice_in_dim(array, 0, width, axis=dim)
        before = lax.ppermute(last, axis, up)
        after = lax.ppermute(first, axis, down)
        array = jnp.concatenate([before, array, after], axis=dim)
    return array


def basis_table():
    taps = jnp.arange(9)
    row_step = taps // 3 - 1
    col_step = taps % 3 - 1
    cycle = jnp.abs(row_step) + jnp.abs(col_step)
    angle = jnp.arctan2(row_step.astype(jnp.float32), col_step.astype(jnp.float32))
    turns = jnp.arange(8).astype(jnp.float32) * (2.0 * math.pi / 8.0)
    rotated = angle[:, None] - turns[None, :]
    cycle_of = jnp.array([0, 1, 1, 1, 1, 1, 1, 1, 1, 2, 2, 2, 2, 2, 2, 2], dtype=jnp.int32)
    freq = jnp.array([0, 0, 1, 1, 2, 2, 3, 3, 4, 0, 1, 1, 2, 2, 3, 3], dtype=jnp.float32)
    sine = jnp.array([0, 0, 0, 1, 0, 1, 0, 1, 0, 0, 0, 1, 0, 1, 0, 1], dtype=jnp.int32)
    phase = rotated[:, :, None] * freq[None, None, :]
    wave = jnp.where(sine[None, None, :] == 1, jnp.sin(phase), jnp.cos(phase))
    return jnp.where(cycle[:, None, None] == cycle_of[None, None, :], wave, jnp.zeros_like(wave))


def rotation_select():
    first = jnp.arange(8)[:, None, None]
    second = jnp.arange(8)[None, :, None]
    offset = jnp.arange(8)[None, None, :]
    return ((second - first) % 8 == offset).astype(jnp.float32)


def mixing_table(table, select):
    joined = table[:, :, None, None, :] * select[None, :, :, :, None]
    return joined.reshape(9, 64, 8 * NB)


def expand(panel, tap_mix):
    out_fields = panel.shape[0]
    in_fields = panel.shape[1] // (8 * NB)
    coeffs = panel.astype(jnp.float32).reshape(out_fields * in_fields, 8 * NB)
    blocks = []
    for tap_index in range(9):
        placed = lax.dot_general(
            coeffs,
            tap_mix[tap_index],
            (((1,), (1,)), ((), ())),
            precision=lax.Precision.HIGHEST,
            preferred_element_type=jnp.float32,
        )
        placed = placed.reshape(out_fields, in_fields, 8, 8).transpose(0, 2, 1, 3)
        blocks.append(placed.reshape(out_fields * 8, in_fields * 8).astype(jnp.bfloat16))
    return jnp.stack(blocks)


def contract(gram, mix_tap):
    out_fields = gram.shape[0] // 8
    in_fields = gram.shape[1] // 8
    blocks = (
        gram.reshape(out_fields, 8, in_fields, 8)
        .transpose(0, 2, 1, 3)
        .reshape(out_fields * in_fields, 64)
    )
    return jnp.dot(
        blocks, mix_tap, precision=lax.Precision.HIGHEST, preferred_element_type=jnp.float32
    )


def convolve(padded, kernel_taps, layout):
    shaped = kernel_taps.reshape(3, 3, kernel_taps.shape[1], kernel_taps.shape[2])
    return lax.conv_general_dilated(
        padded,
        shaped,
        (1, 1),
        ((0, 0), (1, 1)),
        dimension_numbers=("NHWC", layout, "NHWC"),
        preferred_element_type=jnp.float32,
    )


def local(features, cotangent, valid, coefficients):
    tap_mix = mixing_table(basis_table(), rotation_select())
    coef_all = lax.all_gather(coefficients, ("dp", "chan"), axis=1, tiled=True)
    share = FIELDS // lax.axis_size("chan")
    first_field = lax.axis_index("chan") * share
    own_rows = lax.dynamic_slice_in_dim(coef_all, first_field, share, 0)
    kernel_out = expand(own_rows, tap_mix)
    cameras, band_rows, frame_cols, channels = features.shape
    own_channels = share * 8
    masked = cotangent * valid[..., None].astype(jnp.bfloat16)
    stacked = jnp.concatenate([features, masked], axis=3)
    padded = padded_2(stacked, (("space", 1),), 1)
    padded_x = padded[..., :channels]
    padded_g = padded[..., channels:]
    total_out = convolve(padded_x, kernel_out, "HWOI")
    total_back = convolve(padded_g, kernel_out[::-1], "HWIO")
    gram_all = lax.conv_general_dilated(
        padded_x,
        masked,
        (1, 1),
        ((0, 0), (1, 1)),
        dimension_numbers=("CHWN", "IHWO", "NHWC"),
        preferred_element_type=jnp.float32,
    )
    gram_taps = gram_all.reshape(channels, 9, own_channels).transpose(1, 2, 0)
    raw = jnp.zeros((share * FIELDS, 8 * NB), jnp.float32)
    for tap_index in range(9):
        raw = raw + contract(gram_taps[tap_index], tap_mix[tap_index])
    summed = lax.psum_scatter(
        total_back.astype(jnp.bfloat16), "chan", scatter_dimension=3, tiled=True
    )
    raw_flat = raw.reshape(share, FIELDS * 8 * NB)
    shares = lax.psum_scatter(raw_flat, ("space", "dp"), scatter_dimension=1, tiled=True)
    squares = lax.psum(jnp.sum(shares * shares), ("space", "dp", "chan"))
    norm = jnp.sqrt(squares + 1e-06)
    factor = math.sqrt(FIELDS * FIELDS * 8 * NB) / norm
    conv_out = total_out.astype(jnp.bfloat16)
    return (conv_out, summed, shares * factor)


TURNS = (((0, 1), (1, 0), (0, -1), (-1, 0)), ((1, 1), (1, -1), (-1, -1), (-1, 1)))


def mixing_matrix():
    table = np.zeros((3, 8, 8, 8, NB))
    for cycle in range(3):
        for i in range(8):
            psi = 2.0 * math.pi * ((cycle == 2) - i) / 8.0
            waves = np.zeros(NB)
            if cycle == 0:
                waves[0] = 1.0
            else:
                full = [1.0]
                for freq in range(1, 5):
                    full += [math.cos(freq * psi), math.sin(freq * psi)]
                first = 1 if cycle == 1 else 9
                count = 8 if cycle == 1 else 7
                waves[first : first + count] = full[:count]
            for j in range(8):
                table[cycle, i, j, (j - i) % 8] = waves
    return table.reshape(192, 8 * NB).astype(np.float32)


def dot(a, b, dims):
    return lax.dot_general(a, b, ((dims[:1], dims[1:]), ((), ())), preferred_element_type=jnp.float32)


def grid_ids(rows, cols):
    return (
        lax.broadcasted_iota(jnp.int32, (rows, cols), 0),
        lax.broadcasted_iota(jnp.int32, (rows, cols), 1),
    )


def ones_at(cond):
    return jnp.where(cond, 1.0, 0.0).astype(jnp.bfloat16)


def lane_groups(pieces, shape):
    group = lax.broadcasted_iota(jnp.int32, shape, len(shape) - 1) // 32
    out = pieces[0]
    for k in range(1, 4):
        out = jnp.where(group == k, pieces[k], out)
    return out


def rolled(array, groups):
    if groups % 4 == 0:
        return array
    flat = array.reshape(-1, 128)
    return pltpu.roll(flat, 32 * (groups % 4), 1).reshape(array.shape)


def fused_kernel(
    sizes,
    x_ref, g_ref, v_ref, c_ref, mix_ref, mixt_ref,
    out_ref, back_ref, grad_ref,
    xp, mp, cg, xs, blocks, kt, back_own, back_send, back_recv,
    raw_send, raw_recv, sq_send, sq_recv,
    hs_sem, hr_sem, cs_sem, cr_sem, bs_sem, br_sem, rs_sem, rr_sem, ss_sem, sr_sem,
):
    n_space, n_dp, n_chan, rows, cols = sizes
    pix = rows * cols
    space, dp, chan = lax.axis_index("space"), lax.axis_index("dp"), lax.axis_index("chan")
    bf16 = jnp.bfloat16
    n_own = n_space * n_dp
    n_all = n_own * n_chan
    me_own = space * n_dp + dp
    me_all = me_own * n_chan + chan
    me_coef = dp * n_chan + chan
    n_coef = n_dp * n_chan

    def id_all(k):
        o = lax.rem(me_all + k, n_all)
        return {
            "space": o // (n_dp * n_chan),
            "dp": lax.rem(o // n_chan, n_dp),
            "chan": lax.rem(o, n_chan),
        }

    def send(src, dst, ssem, rsem, device):
        return pltpu.make_async_remote_copy(
            src_ref=src, dst_ref=dst, send_sem=ssem, recv_sem=rsem,
            device_id=device, device_id_type=pl.DeviceIdType.MESH,
        )

    barrier = pltpu.get_barrier_semaphore()
    for k in range(1, n_all):
        pl.semaphore_signal(barrier, inc=1, device_id=id_all(k), device_id_type=pl.DeviceIdType.MESH)

    r_id, c_id = grid_ids(256, 256)
    to_rot = ones_at(c_id == lax.rem(r_id, 8) * 32 + r_id // 8)
    r64, c64 = grid_ids(cols, cols)
    valid = v_ref[...].astype(jnp.float32)
    for r in range(rows):
        diag = jnp.where(r64 == c64, jnp.broadcast_to(valid[r : r + 1, :], (cols, cols)), 0.0).astype(bf16)
        row = dot(diag, g_ref[r * cols : (r + 1) * cols, :], (1, 0)).astype(bf16)
        mp[(r + 1) * cols : (r + 2) * cols, :] = dot(row, to_rot, (1, 0)).astype(bf16)

    @pl.when(space == 0)
    def _():
        xp[0:cols, :] = jnp.zeros((cols, 512), bf16)
        mp[0:cols, :] = jnp.zeros((cols, 256), bf16)

    @pl.when(space == n_space - 1)
    def _():
        xp[pix + cols : pix + 2 * cols, :] = jnp.zeros((cols, 512), bf16)
        mp[pix + cols : pix + 2 * cols, :] = jnp.zeros((cols, 256), bf16)

    pl.semaphore_wait(barrier, n_all - 1)

    down = {"space": lax.rem(space + 1, n_space)}
    up = {"space": lax.rem(space + n_space - 1, n_space)}
    lo, hi = pl.ds(0, cols), pl.ds(pix + cols, cols)
    last, first = pl.ds(pix, cols), pl.ds(cols, cols)
    x_down = send(x_ref.at[pl.ds(pix - cols, cols)], xp.at[lo], hs_sem.at[0], hr_sem.at[0], down)
    x_up = send(x_ref.at[pl.ds(0, cols)], xp.at[hi], hs_sem.at[1], hr_sem.at[1], up)
    m_down = send(mp.at[last], mp.at[lo], hs_sem.at[2], hr_sem.at[2], down)
    m_up = send(mp.at[first], mp.at[hi], hs_sem.at[3], hr_sem.at[3], up)

    @pl.when(space < n_space - 1)
    def _():
        x_down.start()
        m_down.start()

    @pl.when(space > 0)
    def _():
        x_up.start()
        m_up.start()

    coef_copies = []
    for k in range(1, n_coef):
        o = lax.rem(me_coef + k, n_coef)
        o_chan = lax.rem(o, n_chan)
        copy = send(
            c_ref.at[pl.ds(pl.multiple_of(o_chan * 32, 32), 32)], cg.at[me_coef],
            cs_sem.at[k], cr_sem.at[k], {"dp": o // n_chan, "chan": o_chan},
        )
        copy.start()
        coef_copies.append(copy)

    xp[cols : pix + cols, :] = x_ref[...]
    cg[me_coef] = c_ref[pl.ds(pl.multiple_of(chan * 32, 32), 32), :]
    shift_next = ones_at(c64 == r64 + 1)
    shift_prev = ones_at(c64 == r64 - 1)
    perms = [None] + [
        ones_at(r_id == (c_id // 8) * 8 + lax.rem(c_id + 2 * turn, 8)) for turn in (1, 2, 3)
    ]

    def wait_halo(a, b):
        @pl.when(space > 0)
        def _():
            a.wait_recv()

        @pl.when(space < n_space - 1)
        def _():
            b.wait_recv()

    wait_halo(x_down, x_up)

    def shifted(ref, row, dc):
        value = ref[row * cols : (row + 1) * cols, :]
        if dc == 0:
            return value
        return dot(shift_next if dc > 0 else shift_prev, value, (1, 0)).astype(bf16)

    for turn in range(4):
        for cycle in range(2):
            dr, dc = TURNS[cycle][turn]
            parts = [shifted(xp, 1 + r + dr, dc) for r in range(rows)]
            value = jnp.concatenate(parts, axis=0)
            for half in range(2):
                piece = value[:, half * 256 : (half + 1) * 256]
                if turn:
                    piece = dot(piece, perms[turn], (1, 0)).astype(bf16)
                xs[cycle, turn * pix : (turn + 1) * pix, half * 256 : (half + 1) * 256] = piece

    def turned(value, turn):
        if turn == 0:
            return value
        return jnp.concatenate([value[:, 64 * turn :], value[:, : 64 * turn]], axis=1)

    own_m = mp[cols : pix + cols, :]
    m_all = jnp.concatenate([turned(own_m, turn) for turn in range(4)], axis=0)
    for cycle in range(3):
        if cycle == 0:
            gram = dot(x_ref[...], own_m, (0, 0))
        else:
            gram = dot(xs[cycle - 1], m_all, (0, 0))
        for half in range(2):
            part = gram[:, half * 128 : (half + 1) * 128].reshape(16, 4, 8, 128)
            turns = [rolled(part, s) for s in range(4)]
            for q in range(4):
                place = lane_groups([turns[(k - q) % 4][:, k] for k in range(4)], (16, 8, 128))
                start = (cycle * 8 + half * 4 + q) * 8
                blocks[:, start : start + 8, :] = place
    per = 16 // n_own
    mixt = mixt_ref[...]
    for group in range(16):
        value = dot(mixt, blocks[group].astype(bf16), (1, 0))
        raw_send[group // per, group % per] = value.astype(bf16)
    raw_copies = []
    for k in range(1, n_own):
        o = lax.rem(me_own + k, n_own)
        copy = send(
            raw_send.at[o], raw_recv.at[me_own], rs_sem.at[k], rr_sem.at[k],
            {"space": o // n_dp, "dp": lax.rem(o, n_dp)},
        )
        copy.start()
        raw_copies.append(copy)
    raw_recv[me_own] = raw_send[me_own]

    for copy in coef_copies:
        copy.wait_recv()
    mix = mix_ref[...]
    per_slot = 64 // n_coef
    for group in range(16):
        stack = []
        for b in range(4 * group, 4 * group + 4):
            lane = (b % per_slot) * 128
            stack.append(cg[b // per_slot, :, lane : lane + 128])
        stack = jnp.concatenate(stack, axis=0)
        blocks[group] = dot(mix, jnp.concatenate([stack, stack], axis=1), (1, 1))
    for cycle in range(3):
        for half in range(2):
            source = []
            for q in range(4):
                start = (cycle * 8 + half * 4 + q) * 8
                part = blocks[:, start : start + 8, :]
                source.append([rolled(part, s) for s in range(4)])
            fields = [
                lane_groups([source[q][(q - k) % 4] for q in range(4)], (16, 8, 128)) for k in range(4)
            ]
            value = jnp.stack(fields, axis=1).reshape(512, 128).astype(bf16)
            kt[cycle, :, half * 128 : (half + 1) * 128] = value

    wait_halo(m_down, m_up)
    lane = lax.broadcasted_iota(jnp.int32, (pix, 512), 1)
    low = lax.rem(lane, 8) < 2
    total = None
    for turn in (3, 2, 1, 0):
        if total is not None:
            total = jnp.where(low, pltpu.roll(total, 512 - 6, 1), pltpu.roll(total, 2, 1))
        for cycle in range(2):
            dr, dc = TURNS[cycle][turn]
            parts = [shifted(mp, 1 + r - dr, -dc) for r in range(rows)]
            value = turned(jnp.concatenate(parts, axis=0), turn)
            term = dot(value, kt[cycle + 1], (1, 1))
            total = term if total is None else total + term
    total = total + dot(own_m, kt[0], (1, 1))
    left, right = total[:, :256], total[:, 256:]
    is_first = chan == 0
    back_own[...] = jnp.where(is_first, left, right)
    back_send[...] = jnp.where(is_first, right, left).astype(bf16)
    back_copy = send(back_send, back_recv, bs_sem, br_sem, {"chan": 1 - chan})
    back_copy.start()

    for copy in raw_copies:
        copy.wait_recv()
    summed = raw_recv[0].astype(jnp.float32)
    for k in range(1, n_own):
        summed = summed + raw_recv[k].astype(jnp.float32)
    sq_send[...] = jnp.sum((summed * summed).reshape(per * 16, 8, 128), axis=0)
    sq_copies = []
    for k in range(1, n_all):
        copy = send(sq_send, sq_recv.at[me_all], ss_sem.at[k], sr_sem.at[k], id_all(k))
        copy.start()
        sq_copies.append(copy)
    sq_recv[me_all] = sq_send[...]

    conv = dot(x_ref[...], kt[0], (1, 0))
    for turn in range(4):
        at = slice(turn * pix, (turn + 1) * pix)
        term = dot(xs[0, at, :], kt[1], (1, 0)) + dot(xs[1, at, :], kt[2], (1, 0))
        conv = conv + (pltpu.roll(term, 64 * turn, 1) if turn else term)
    out_ref[...] = dot(conv.astype(bf16), to_rot, (1, 1)).astype(bf16)

    back_copy.wait_recv()
    back_ref[...] = (back_own[...] + back_recv[...].astype(jnp.float32)).astype(bf16)

    flipped = [summed[g].T for g in range(per)]
    for copy in sq_copies:
        copy.wait_recv()
    squares = jnp.sum(jnp.sum(sq_recv[...], axis=0), keepdims=True)
    factor = math.sqrt(FIELDS * FIELDS * 8 * NB) / jnp.sqrt(squares + 1e-06)
    for b in range(4 * per):
        grad_ref[:, b * 128 : (b + 1) * 128] = flipped[b // 4][(b % 4) * 32 : (b % 4 + 1) * 32, :] * factor

    @pl.when(space < n_space - 1)
    def _():
        x_down.wait_send()
        m_down.wait_send()

    @pl.when(space > 0)
    def _():
        x_up.wait_send()
        m_up.wait_send()

    for copy in coef_copies + raw_copies + sq_copies + [back_copy]:
        copy.wait_send()


def fused(sizes, features, cotangent, valid, coefficients):
    n_space, n_dp, n_chan, rows, cols = sizes
    pix = rows * cols
    n_own, n_coef = n_space * n_dp, n_dp * n_chan
    n_all = n_own * n_chan
    per = 16 // n_own
    bf16, f32 = jnp.bfloat16, jnp.float32
    table = mixing_matrix()
    high = table.astype(bf16)
    low = (table - high.astype(np.float32)).astype(bf16)
    mix = jnp.asarray(np.concatenate([high, low], axis=1))
    mixt = jnp.asarray(np.ascontiguousarray(high.T))
    vmem = pl.BlockSpec(memory_space=pltpu.VMEM)
    dma = pltpu.SemaphoreType.DMA
    out, back, grad = pl.pallas_call(
        functools.partial(fused_kernel, sizes),
        out_shape=(
            jax.ShapeDtypeStruct((pix, 256), bf16),
            jax.ShapeDtypeStruct((pix, 256), bf16),
            jax.ShapeDtypeStruct((32, per * 512), f32),
        ),
        in_specs=[vmem] * 6,
        out_specs=[vmem] * 3,
        scratch_shapes=[
            pltpu.VMEM((pix + 2 * cols, 512), bf16),
            pltpu.VMEM((pix + 2 * cols, 256), bf16),
            pltpu.VMEM((n_coef, 32, coefficients.shape[1]), bf16),
            pltpu.VMEM((2, 4 * pix, 512), bf16),
            pltpu.VMEM((16, 192, 128), f32),
            pltpu.VMEM((3, 512, 256), bf16),
            pltpu.VMEM((pix, 256), f32),
            pltpu.VMEM((pix, 256), bf16),
            pltpu.VMEM((pix, 256), bf16),
            pltpu.VMEM((n_own, per, 128, 128), bf16),
            pltpu.VMEM((n_own, per, 128, 128), bf16),
            pltpu.VMEM((8, 128), f32),
            pltpu.VMEM((n_all, 8, 128), f32),
            dma((4,)), dma((4,)),
            dma((n_coef,)), dma((n_coef,)),
            dma, dma,
            dma((n_own,)), dma((n_own,)),
            dma((n_all,)), dma((n_all,)),
        ],
        compiler_params=pltpu.CompilerParams(
            collective_id=0, has_side_effects=True, vmem_limit_bytes=48 * 1024 * 1024
        ),
    )(
        features.reshape(pix, 512),
        cotangent.reshape(pix, 256),
        valid.reshape(rows, cols),
        coefficients,
        mix,
        mixt,
    )
    shape = (1, rows, cols, 256)
    return out.reshape(shape), back.reshape(shape), grad


def block(features, cotangent, valid, coefficients):
    n_space, n_dp, n_chan = (lax.axis_size(a) for a in ("space", "dp", "chan"))
    cameras, rows, cols, _ = features.shape
    owners = n_space * n_dp
    if cameras == 1 and n_chan == 2 and owners <= 16 and 16 % owners == 0 and cols % 16 == 0 and owners > 1:
        sizes = (n_space, n_dp, n_chan, rows, cols)
        return fused(sizes, features, cotangent, valid, coefficients)
    return local(features, cotangent, valid, coefficients)


def solution(mesh):
    in_specs = (
        P(("parts", "dp"), "space", None, None),
        P(("parts", "dp"), "space", None, "chan"),
        P(("parts", "dp"), "space", None),
        P(None, ("dp", "chan")),
    )
    out_specs = (
        P(("parts", "dp"), "space", None, "chan"),
        P(("parts", "dp"), "space", None, "chan"),
        P(("parts", "chan"), ("space", "dp")),
    )
    return jax.shard_map(block, mesh=mesh, in_specs=in_specs, out_specs=out_specs, check_vma=False)
```

profile of v0, /device:TPU:0, one launch (start us, length us, event | category | flops | bytes accessed | tf_op | source)
XLA Modules:
  0.0 38.9 jit_solution(18385376994726843339)
XLA Ops:
  0.6 0.0 copy-start.5
  0.6 0.7 %copy-done.5 = s32[1,4,64]{2,1,0:T(4,128)S(1)} copy-done((s32[1,4,64]{2,1,0:T(4,128)S(1)}, s32[1,4,64]{2,1,0:T(4,128)}, u32[]{:S(2)}) %copy-start.5) | copy-done | bytes 1048
  1.3 0.0 copy-start
  1.3 0.9 %copy-done = bf16[1,4,64,512]{3,2,1,0:T(8,128)(2,1)S(1)} copy-done((bf16[1,4,64,512]{3,2,1,0:T(8,128)(2,1)S(1)}, bf16[1,4,64,512]{3,2,1,0:T(8,128)(2,1)}, u32[]{:S(2)}) %copy-start) | copy-done | bytes 262168
  2.3 0.0 copy-start.1
  2.3 0.9 %copy-done.1 = bf16[64,2048]{1,0:T(8,128)(2,1)S(1)} copy-done((bf16[64,2048]{1,0:T(8,128)(2,1)S(1)}, bf16[64,2048]{1,0:T(8,128)(2,1)}, u32[]{:S(2)}) %copy-start.1) | copy-done | bytes 262168
  3.2 0.0 copy-start.2
  3.2 0.9 %copy-done.2 = bf16[1,4,64,256]{3,2,1,0:T(8,128)(2,1)S(1)} copy-done((bf16[1,4,64,256]{3,2,1,0:T(8,128)(2,1)S(1)}, bf16[1,4,64,256]{3,2,1,0:T(8,128)(2,1)}, u32[]{:S(2)}) %copy-start.2) | copy-done | bytes 131096
  4.1 0.0 copy-start.3
  4.1 0.9 %copy-done.3 = bf16[192,256]{1,0:T(8,128)(2,1)S(1)} copy-done((bf16[192,256]{1,0:T(8,128)(2,1)S(1)}, bf16[192,256]{1,0:T(8,128)(2,1)}, u32[]{:S(2)}) %copy-start.3) | copy-done | bytes 98328
  5.0 0.0 copy-start.4
  5.0 0.8 %copy-done.4 = bf16[128,192]{1,0:T(8,128)(2,1)S(1)} copy-done((bf16[128,192]{1,0:T(8,128)(2,1)S(1)}, bf16[128,192]{1,0:T(8,128)(2,1)}, u32[]{:S(2)}) %copy-start.4) | copy-done | bytes 49176
  5.9 31.1 %shard_map.85 = (bf16[256,256]{1,0:T(8,128)(2,1)S(1)}, bf16[256,256]{1,0:T(8,128)(2,1)S(1)}, f32[32,1024]{1,0:T(8,128)S(1)}) custom-call(bf16[256,512]{1,0:T(8,128)(2,1)S(1)} %bitcast.5, bf16[256,256]{1,0:T(8,128)(2,1)S(1)} %bitcast.6, s32[4,64]{1,0:T(4,128)S(1)} %bitcast.9, bf16[64,2048]{1,0:T(8,128)(2,1)S(1)} %copy-done.1, bf16[192,256]{1,0:T(8,128)(2,1)S(1)} %copy-done.3, ...), custom_call_target="tpu_custom_call" | custom-call | tf_op jit(solution)/shard_map/pallas_call | solution.py:456
  37.0 0.7 %copy.12 = bf16[1,4,64,256]{3,2,1,0:T(8,128)(2,1)} copy(bf16[1,4,64,256]{3,2,1,0:T(8,128)(2,1)S(1)} %bitcast.8) | data formatting | bytes 262144
  37.6 0.7 %copy.13 = bf16[1,4,64,256]{3,2,1,0:T(8,128)(2,1)} copy(bf16[1,4,64,256]{3,2,1,0:T(8,128)(2,1)S(1)} %bitcast.7) | data formatting | bytes 262144
  38.3 0.7 %copy.14 = f32[32,1024]{1,0:T(8,128)} copy(f32[32,1024]{1,0:T(8,128)S(1)} %get-tuple-element.14) | data formatting | bytes 262144
Async XLA Ops:
  0.6 0.7 %copy-start.5 = (s32[1,4,64]{2,1,0:T(4,128)S(1)}, s32[1,4,64]{2,1,0:T(4,128)}, u32[]{:S(2)}) copy-start(s32[1,4,64]{2,1,0:T(4,128)} %param.8) | copy-start | bytes 3076
  1.3 0.9 %copy-start = (bf16[1,4,64,512]{3,2,1,0:T(8,128)(2,1)S(1)}, bf16[1,4,64,512]{3,2,1,0:T(8,128)(2,1)}, u32[]{:S(2)}) copy-start(bf16[1,4,64,512]{3,2,1,0:T(8,128)(2,1)} %param.6) | copy-start | bytes 786436
  2.3 0.9 %copy-start.1 = (bf16[64,2048]{1,0:T(8,128)(2,1)S(1)}, bf16[64,2048]{1,0:T(8,128)(2,1)}, u32[]{:S(2)}) copy-start(bf16[64,2048]{1,0:T(8,128)(2,1)} %c_ref.1) | copy-start | bytes 786436
  3.2 0.9 %copy-start.2 = (bf16[1,4,64,256]{3,2,1,0:T(8,128)(2,1)S(1)}, bf16[1,4,64,256]{3,2,1,0:T(8,128)(2,1)}, u32[]{:S(2)}) copy-start(bf16[1,4,64,256]{3,2,1,0:T(8,128)(2,1)} %param.7) | copy-start | bytes 393220
  4.1 0.9 %copy-start.3 = (bf16[192,256]{1,0:T(8,128)(2,1)S(1)}, bf16[192,256]{1,0:T(8,128)(2,1)}, u32[]{:S(2)}) copy-start(bf16[192,256]{1,0:T(8,128)(2,1)} %constant.4.clone.mix_ref) | copy-start | bytes 294916
  5.0 0.8 %copy-start.4 = (bf16[128,192]{1,0:T(8,128)(2,1)S(1)}, bf16[128,192]{1,0:T(8,128)(2,1)}, u32[]{:S(2)}) copy-start(bf16[128,192]{1,0:T(8,128)(2,1)} %constant.5.clone.mixt_ref) | copy-start | bytes 147460
where the time goes:
time: 39.2 us; the launch traced here: 38.9 us
  Pallas kernels  31.1 us (79%)
  local copies, waits for them, and re-layouts  7.18 us (18%)
  between operations  0.65 us (2%)
    pallas_call x1, Pallas kernels, fused(): pl.pallas_call(functools.partial(fused_kernel, sizes), out_shape=(jax.Sha...  31.1 us
    unnamed x15, local copies, waits for them, and re-layouts  7.18 us

commit v1 on v0

--- a/solution.py
+++ b/solution.py
@@ -192,10 +192,12 @@
 
 def fused_kernel(
     sizes,
-    x_ref, g_ref, v_ref, c_ref, mix_ref, mixt_ref,
+    x_hbm, g_hbm, v_hbm, c_hbm, mix_hbm, mixt_hbm,
     out_ref, back_ref, grad_ref,
     xp, mp, cg, xs, blocks, kt, back_own, back_send, back_recv,
     raw_send, raw_recv, sq_send, sq_recv,
+    g_ref, v_ref, c_ref, mix_ref, mixt_ref, in_sem,
+    own_raw, z_send, z_recv, kblocks, ps_sem, pr_sem,
     hs_sem, hr_sem, cs_sem, cr_sem, bs_sem, br_sem, rs_sem, rr_sem, ss_sem, sr_sem,
 ):
     n_space, n_dp, n_chan, rows, cols = sizes
@@ -209,13 +211,20 @@
     me_coef = dp * n_chan + chan
     n_coef = n_dp * n_chan
 
-    def id_all(k):
-        o = lax.rem(me_all + k, n_all)
-        return {
-            "space": o // (n_dp * n_chan),
-            "dp": lax.rem(o // n_chan, n_dp),
-            "chan": lax.rem(o, n_chan),
-        }
+    def step(index, k, size):
+        moved = index + k
+        return jnp.where(moved >= size, moved - size, moved)
+
+    peers = [
+        (ks, kd, kc)
+        for ks in range(n_space)
+        for kd in range(n_dp)
+        for kc in range(n_chan)
+        if ks or kd or kc
+    ]
+
+    def device(ks, kd, kc):
+        return {"space": step(space, ks, n_space), "dp": step(dp, kd, n_dp), "chan": step(chan, kc, n_chan)}
 
     def send(src, dst, ssem, rsem, device):
         return pltpu.make_async_remote_copy(
@@ -223,13 +232,33 @@
             device_id=device, device_id_type=pl.DeviceIdType.MESH,
         )
 
+    loads = [
+        pltpu.make_async_copy(src, dst, in_sem.at[k])
+        for k, (src, dst) in enumerate(
+            (
+                (v_hbm, v_ref),
+                (g_hbm, g_ref),
+                (x_hbm, xp.at[pl.ds(cols, pix)]),
+                (mixt_hbm, mixt_ref),
+                (c_hbm.at[pl.ds(pl.multiple_of(chan * 32, 32), 32)], c_ref),
+                (mix_hbm, mix_ref),
+            )
+        )
+    ]
+    for load in loads:
+        load.start()
+
     barrier = pltpu.get_barrier_semaphore()
-    for k in range(1, n_all):
-        pl.semaphore_signal(barrier, inc=1, device_id=id_all(k), device_id_type=pl.DeviceIdType.MESH)
+    for peer in peers:
+        pl.semaphore_signal(
+            barrier, inc=1, device_id=device(*peer), device_id_type=pl.DeviceIdType.MESH
+        )
 
     r_id, c_id = grid_ids(256, 256)
     to_rot = ones_at(c_id == lax.rem(r_id, 8) * 32 + r_id // 8)
     r64, c64 = grid_ids(cols, cols)
+    loads[0].wait()
+    loads[1].wait()
     valid = v_ref[...].astype(jnp.float32)
     for r in range(rows):
         diag = jnp.where(r64 == c64, jnp.broadcast_to(valid[r : r + 1, :], (cols, cols)), 0.0).astype(bf16)
@@ -248,12 +277,12 @@
 
     pl.semaphore_wait(barrier, n_all - 1)
 
-    down = {"space": lax.rem(space + 1, n_space)}
-    up = {"space": lax.rem(space + n_space - 1, n_space)}
+    down = {"space": step(space, 1, n_space)}
+    up = {"space": step(space, n_space - 1, n_space)}
     lo, hi = pl.ds(0, cols), pl.ds(pix + cols, cols)
     last, first = pl.ds(pix, cols), pl.ds(cols, cols)
-    x_down = send(x_ref.at[pl.ds(pix - cols, cols)], xp.at[lo], hs_sem.at[0], hr_sem.at[0], down)
-    x_up = send(x_ref.at[pl.ds(0, cols)], xp.at[hi], hs_sem.at[1], hr_sem.at[1], up)
+    x_down = send(x_hbm.at[pl.ds(pix - cols, cols)], xp.at[lo], hs_sem.at[0], hr_sem.at[0], down)
+    x_up = send(x_hbm.at[pl.ds(0, cols)], xp.at[hi], hs_sem.at[1], hr_sem.at[1], up)
     m_down = send(mp.at[last], mp.at[lo], hs_sem.at[2], hr_sem.at[2], down)
     m_up = send(mp.at[first], mp.at[hi], hs_sem.at[3], hr_sem.at[3], up)
 
@@ -269,17 +298,15 @@
 
     coef_copies = []
     for k in range(1, n_coef):
-        o = lax.rem(me_coef + k, n_coef)
-        o_chan = lax.rem(o, n_chan)
+        kd, kc = divmod(k, n_chan)
+        o_chan = step(chan, kc, n_chan)
         copy = send(
-            c_ref.at[pl.ds(pl.multiple_of(o_chan * 32, 32), 32)], cg.at[me_coef],
-            cs_sem.at[k], cr_sem.at[k], {"dp": o // n_chan, "chan": o_chan},
+            c_hbm.at[pl.ds(pl.multiple_of(o_chan * 32, 32), 32)], cg.at[me_coef],
+            cs_sem.at[k], cr_sem.at[k], {"dp": step(dp, kd, n_dp), "chan": o_chan},
         )
         copy.start()
         coef_copies.append(copy)
 
-    xp[cols : pix + cols, :] = x_ref[...]
-    cg[me_coef] = c_ref[pl.ds(pl.multiple_of(chan * 32, 32), 32), :]
     shift_next = ones_at(c64 == r64 + 1)
     shift_prev = ones_at(c64 == r64 - 1)
     perms = [None] + [
@@ -295,6 +322,7 @@
         def _():
             b.wait_recv()
 
+    loads[2].wait()
     wait_halo(x_down, x_up)
 
     def shifted(ref, row, dc):
@@ -323,7 +351,7 @@
     m_all = jnp.concatenate([turned(own_m, turn) for turn in range(4)], axis=0)
     for cycle in range(3):
         if cycle == 0:
-            gram = dot(x_ref[...], own_m, (0, 0))
+            gram = dot(xp[cols : pix + cols, :], own_m, (0, 0))
         else:
             gram = dot(xs[cycle - 1], m_all, (0, 0))
         for half in range(2):
@@ -334,21 +362,32 @@
                 start = (cycle * 8 + half * 4 + q) * 8
                 blocks[:, start : start + 8, :] = place
     per = 16 // n_own
+    loads[3].wait()
     mixt = mixt_ref[...]
-    for group in range(16):
-        value = dot(mixt, blocks[group].astype(bf16), (1, 0))
-        raw_send[group // per, group % per] = value.astype(bf16)
-    raw_copies = []
-    for k in range(1, n_own):
-        o = lax.rem(me_own + k, n_own)
-        copy = send(
-            raw_send.at[o], raw_recv.at[me_own], rs_sem.at[k], rr_sem.at[k],
-            {"space": o // n_dp, "dp": lax.rem(o, n_dp)},
-        )
-        copy.start()
-        raw_copies.append(copy)
-    raw_recv[me_own] = raw_send[me_own]
-
+
+    def mixed(owner, g):
+        return dot(mixt, blocks[owner * per + g].astype(bf16), (1, 0))
+
+    order = sorted(range(n_space), key=lambda k: -min(k, n_space - k))
+    dp_copies, raw_copies = [], []
+    for ks in order:
+        to_space = step(space, ks, n_space)
+        for kd in range(1, n_dp):
+            to_dp = step(dp, kd, n_dp)
+            for g in range(per):
+                raw_send[ks, kd, g] = mixed(to_space * n_dp + to_dp, g).astype(bf16)
+            at = (ks, kd)
+            copy = send(raw_send.at[at], raw_recv.at[at], ps_sem.at[at], pr_sem.at[at], {"dp": to_dp})
+            copy.start()
+            dp_copies.append((ks, copy))
+    for ks in order:
+        to_space = step(space, ks, n_space)
+        for g in range(per):
+            own_raw[ks, g] = mixed(to_space * n_dp + dp, g)
+
+    loads[4].wait()
+    loads[5].wait()
+    cg[me_coef] = c_ref[...]
     for copy in coef_copies:
         copy.wait_recv()
     mix = mix_ref[...]
@@ -359,13 +398,30 @@
             lane = (b % per_slot) * 128
             stack.append(cg[b // per_slot, :, lane : lane + 128])
         stack = jnp.concatenate(stack, axis=0)
-        blocks[group] = dot(mix, jnp.concatenate([stack, stack], axis=1), (1, 1))
+        kblocks[group] = dot(mix, jnp.concatenate([stack, stack], axis=1), (1, 1))
+    for ks in order:
+        for at, copy in dp_copies:
+            if at == ks:
+                copy.wait_recv()
+        value = own_raw[ks]
+        for kd in range(1, n_dp):
+            value = value + raw_recv[ks, kd].astype(jnp.float32)
+        if ks == 0:
+            own_raw[0] = value
+        else:
+            z_send[ks] = value.astype(bf16)
+            copy = send(
+                z_send.at[ks], z_recv.at[ks], rs_sem.at[ks], rr_sem.at[ks],
+                {"space": step(space, ks, n_space)},
+            )
+            copy.start()
+            raw_copies.append(copy)
     for cycle in range(3):
         for half in range(2):
             source = []
             for q in range(4):
                 start = (cycle * 8 + half * 4 + q) * 8
-                part = blocks[:, start : start + 8, :]
+                part = kblocks[:, start : start + 8, :]
                 source.append([rolled(part, s) for s in range(4)])
             fields = [
                 lane_groups([source[q][(q - k) % 4] for q in range(4)], (16, 8, 128)) for k in range(4)
@@ -394,24 +450,24 @@
     back_copy = send(back_send, back_recv, bs_sem, br_sem, {"chan": 1 - chan})
     back_copy.start()
 
-    for copy in raw_copies:
-        copy.wait_recv()
-    summed = raw_recv[0].astype(jnp.float32)
-    for k in range(1, n_own):
-        summed = summed + raw_recv[k].astype(jnp.float32)
-    sq_send[...] = jnp.sum((summed * summed).reshape(per * 16, 8, 128), axis=0)
-    sq_copies = []
-    for k in range(1, n_all):
-        copy = send(sq_send, sq_recv.at[me_all], ss_sem.at[k], sr_sem.at[k], id_all(k))
-        copy.start()
-        sq_copies.append(copy)
-    sq_recv[me_all] = sq_send[...]
-
-    conv = dot(x_ref[...], kt[0], (1, 0))
+    conv = dot(xp[cols : pix + cols, :], kt[0], (1, 0))
     for turn in range(4):
         at = slice(turn * pix, (turn + 1) * pix)
         term = dot(xs[0, at, :], kt[1], (1, 0)) + dot(xs[1, at, :], kt[2], (1, 0))
         conv = conv + (pltpu.roll(term, 64 * turn, 1) if turn else term)
+    for copy in raw_copies:
+        copy.wait_recv()
+    summed = own_raw[0]
+    for ks in range(1, n_space):
+        summed = summed + z_recv[ks].astype(jnp.float32)
+    sq_send[...] = jnp.sum((summed * summed).reshape(per * 16, 8, 128), axis=0)
+    sq_copies = []
+    for k, peer in enumerate(peers):
+        copy = send(sq_send, sq_recv.at[me_all], ss_sem.at[k], sr_sem.at[k], device(*peer))
+        copy.start()
+        sq_copies.append(copy)
+    sq_recv[me_all] = sq_send[...]
+
     out_ref[...] = dot(conv.astype(bf16), to_rot, (1, 1)).astype(bf16)
 
     back_copy.wait_recv()
@@ -435,7 +491,7 @@
         x_up.wait_send()
         m_up.wait_send()
 
-    for copy in coef_copies + raw_copies + sq_copies + [back_copy]:
+    for copy in coef_copies + [c for _, c in dp_copies] + raw_copies + sq_copies + [back_copy]:
         copy.wait_send()
 
 
@@ -460,7 +516,7 @@
             jax.ShapeDtypeStruct((pix, 256), bf16),
             jax.ShapeDtypeStruct((32, per * 512), f32),
         ),
-        in_specs=[vmem] * 6,
+        in_specs=[pl.BlockSpec(memory_space=pltpu.HBM)] * 6,
         out_specs=[vmem] * 3,
         scratch_shapes=[
             pltpu.VMEM((pix + 2 * cols, 512), bf16),
@@ -472,18 +528,29 @@
             pltpu.VMEM((pix, 256), f32),
             pltpu.VMEM((pix, 256), bf16),
             pltpu.VMEM((pix, 256), bf16),
-            pltpu.VMEM((n_own, per, 128, 128), bf16),
-            pltpu.VMEM((n_own, per, 128, 128), bf16),
+            pltpu.VMEM((n_space, n_dp, per, 128, 128), bf16),
+            pltpu.VMEM((n_space, n_dp, per, 128, 128), bf16),
             pltpu.VMEM((8, 128), f32),
             pltpu.VMEM((n_all, 8, 128), f32),
+            pltpu.VMEM((pix, 256), bf16),
+            pltpu.VMEM((rows, cols), jnp.int32),
+            pltpu.VMEM((32, coefficients.shape[1]), bf16),
+            pltpu.VMEM(mix.shape, bf16),
+            pltpu.VMEM(mixt.shape, bf16),
+            dma((6,)),
+            pltpu.VMEM((n_space, per, 128, 128), f32),
+            pltpu.VMEM((n_space, per, 128, 128), bf16),
+            pltpu.VMEM((n_space, per, 128, 128), bf16),
+            pltpu.VMEM((16, 192, 128), f32),
+            dma((n_space, n_dp)), dma((n_space, n_dp)),
             dma((4,)), dma((4,)),
             dma((n_coef,)), dma((n_coef,)),
             dma, dma,
-            dma((n_own,)), dma((n_own,)),
+            dma((n_space,)), dma((n_space,)),
             dma((n_all,)), dma((n_all,)),
         ],
         compiler_params=pltpu.CompilerParams(
-            collective_id=0, has_side_effects=True, vmem_limit_bytes=48 * 1024 * 1024
+            collective_id=0, has_side_effects=True, vmem_limit_bytes=63 * 1024 * 1024
         ),
     )(
         features.reshape(pix, 512),

time: 39.2 us -> 33.1 us (0.84)
  local copies, waits for them, and re-layouts: 7.18 us -> 3.21 us
  Pallas kernels: 31.1 us -> 29 us
    unnamed x15 -> x7, local copies, waits for them, and re-layouts: 7.18 us -> 3.21 us
    pallas_call x1, Pallas kernels: 31.1 us -> 29 us  [fused(): pl.pallas_call(functools.partial(fused_kernel, sizes), out_shape=(jax.Sha...]
where the time goes in v1:
time: 33.1 us; the launch traced here: 32.9 us
  Pallas kernels  29 us (88%)
  local copies, waits for them, and re-layouts  3.21 us (10%)
  between operations  0.65 us (2%)
    pallas_call x1, Pallas kernels, fused(): pl.pallas_call(functools.partial(fused_kernel, sizes), out_shape=(jax.Sha...  29 us
    unnamed x7, local copies, waits for them, and re-layouts  3.21 us

profile of v1, /device:TPU:0, one launch (start us, length us, event | category | flops | bytes accessed | tf_op | source)
XLA Modules:
  0.0 32.9 jit_solution(5690851110690597362)
XLA Ops:
  0.6 29.0 %shard_map.85 = (bf16[256,256]{1,0:T(8,128)(2,1)}, bf16[256,256]{1,0:T(8,128)(2,1)}, f32[32,1024]{1,0:T(8,128)}) custom-call(bf16[256,512]{1,0:T(8,128)(2,1)} %bitcast.5, bf16[256,256]{1,0:T(8,128)(2,1)} %bitcast.6, s32[4,64]{1,0:T(4,128)} %bitcast.9, bf16[64,2048]{1,0:T(8,128)(2,1)} %c_hbm.1, bf16[192,256]{1,0:T(8,128)(2,1)} %constant.4.clone.mix_hbm, ...), custom_call_target="tpu_custom_call" | custom-call | tf_op jit(solution)/shard_map/pallas_call | solution.py:512
  29.7 0.0 copy-start.1
  29.7 1.6 %copy.12 = bf16[1,4,64,256]{3,2,1,0:T(8,128)(2,1)} copy(bf16[1,4,64,256]{3,2,1,0:T(8,128)(2,1)} %bitcast.8) | data formatting | bytes 262144
  31.3 0.0 copy-done.1
  31.3 0.0 copy-start
  31.3 0.7 %copy.13 = bf16[1,4,64,256]{3,2,1,0:T(8,128)(2,1)} copy(bf16[1,4,64,256]{3,2,1,0:T(8,128)(2,1)S(1)} %bitcast.7) | data formatting | bytes 262144
  31.9 0.3 copy-done
  32.2 0.7 %copy.14 = f32[32,1024]{1,0:T(8,128)} copy(f32[32,1024]{1,0:T(8,128)S(1)} %copy-done) | data formatting | bytes 262144
Async XLA Ops:
  29.7 1.6 %copy-start.1 = (bf16[256,256]{1,0:T(8,128)(2,1)S(1)}, bf16[256,256]{1,0:T(8,128)(2,1)}, u32[]{:S(2)}) copy-start(bf16[256,256]{1,0:T(8,128)(2,1)} %get-tuple-element.7) | copy-start | bytes 393220
  31.3 1.0 %copy-start = (f32[32,1024]{1,0:T(8,128)S(1)}, f32[32,1024]{1,0:T(8,128)}, u32[]{:S(2)}) copy-start(f32[32,1024]{1,0:T(8,128)} %get-tuple-element.14) | copy-start | bytes 393220

commit v2 on v1

--- a/solution.py
+++ b/solution.py
@@ -493,6 +493,22 @@
 
     for copy in coef_copies + [c for _, c in dp_copies] + raw_copies + sq_copies + [back_copy]:
         copy.wait_send()
+
+
+def hand_on(a, b, c, a_out, b_out, c_out, a_mid, b_mid, c_mid, in_sem, out_sem):
+    mids = (a_mid, b_mid, c_mid)
+    loads = [pltpu.make_async_copy(src, mid, in_sem.at[k]) for k, (src, mid) in enumerate(zip((a, b, c), mids))]
+    stores = [
+        pltpu.make_async_copy(mid, dst, out_sem.at[k])
+        for k, (mid, dst) in enumerate(zip(mids, (a_out, b_out, c_out)))
+    ]
+    for load in loads:
+        load.start()
+    for load, store in zip(loads, stores):
+        load.wait()
+        store.start()
+    for store in stores:
+        store.wait()
 
 
 def fused(sizes, features, cotangent, valid, coefficients):
@@ -560,6 +576,15 @@
         mix,
         mixt,
     )
+    hbm = pl.BlockSpec(memory_space=pltpu.HBM)
+    out, back, grad = pl.pallas_call(
+        hand_on,
+        out_shape=tuple(jax.ShapeDtypeStruct(a.shape, a.dtype) for a in (out, back, grad)),
+        in_specs=[hbm] * 3,
+        out_specs=[hbm] * 3,
+        scratch_shapes=[pltpu.VMEM(a.shape, a.dtype) for a in (out, back, grad)] + [dma((3,)), dma((3,))],
+        compiler_params=pltpu.CompilerParams(vmem_limit_bytes=63 * 1024 * 1024),
+    )(out, back, grad)
     shape = (1, rows, cols, 256)
     return out.reshape(shape), back.reshape(shape), grad
 

time: 33.1 us -> 31.5 us (0.952)
  local copies, waits for them, and re-layouts: 3.21 us -> 0 us
  Pallas kernels: 29 us -> 30.7 us
    unnamed x7 -> x0, local copies, waits for them, and re-layouts: 3.21 us -> none
    pallas_call x0 -> x1, Pallas kernels: none -> 1.74 us  [fused(): pl.pallas_call(hand_on, out_shape=tuple((jax.ShapeDtypeStruct(a.shape, a....]
where the time goes in v2:
time: 31.5 us; the launch traced here: 31.4 us
  Pallas kernels  30.7 us (97%)
  between operations  0.64 us (2%)
    pallas_call x1, Pallas kernels, fused(): pl.pallas_call(functools.partial(fused_kernel, sizes), out_shape=(jax.Sha...  29 us
    pallas_call x1, Pallas kernels, fused(): pl.pallas_call(hand_on, out_shape=tuple((jax.ShapeDtypeStruct(a.shape, a....  1.74 us

profile of v2, /device:TPU:0, one launch (start us, length us, event | category | flops | bytes accessed | tf_op | source)
XLA Modules:
  0.0 31.4 jit_solution(155747322176788695)
XLA Ops:
  0.6 29.0 %shard_map.85 = (bf16[256,256]{1,0:T(8,128)(2,1)}, bf16[256,256]{1,0:T(8,128)(2,1)}, f32[32,1024]{1,0:T(8,128)}) custom-call(bf16[256,512]{1,0:T(8,128)(2,1)} %bitcast.5, bf16[256,256]{1,0:T(8,128)(2,1)} %bitcast.6, s32[4,64]{1,0:T(4,128)} %bitcast.7, bf16[64,2048]{1,0:T(8,128)(2,1)} %c_hbm.1, bf16[192,256]{1,0:T(8,128)(2,1)} %constant.4.clone.mix_hbm, ...), custom_call_target="tpu_custom_call" | custom-call | tf_op jit(solution)/shard_map/pallas_call | solution.py:528
  29.6 1.7 %shard_map.86 = (bf16[256,256]{1,0:T(8,128)(2,1)}, bf16[256,256]{1,0:T(8,128)(2,1)}, f32[32,1024]{1,0:T(8,128)}) custom-call(bf16[256,256]{1,0:T(8,128)(2,1)} %get-tuple-element.9.a, bf16[256,256]{1,0:T(8,128)(2,1)} %get-tuple-element.10.b, f32[32,1024]{1,0:T(8,128)} %get-tuple-element.11.c), custom_call_target="tpu_custom_call" | custom-call | tf_op jit(solution)/shard_map/pallas_call | solution.py:580
